TPU v7x, 512 devices: a whole 4x4x16 slice. The times are simulated.
512 devices in a mesh: dx: 16 (over y, x), dy: 32 (over z, core).
Axes of the slice: x: 4, y: 4, z: 16, core: 2. Of those that a mesh axis runs over, the one named last changes fastest.
Arguments:
- audio: bfloat16 [32, 128, 2570], P('dy', 'dx'), may hold values from -6 to 6
- counts: int32 [32, 16], P('dy', 'dx'), may hold values from 1 to 8, 64 in all within a row
- cotangent: bfloat16 [32, 64, 256, 512], P('dy', 'dx'), may hold values from -6 to 6
- conv_first: bfloat16 [10, 512], replicated, may hold values from -2 to 2
- norm_gain: float32 [512], replicated, may hold values from 0.1 to 1.9
- norm_bias: float32 [512], replicated, may hold values from -3 to 3
- conv_second: bfloat16 [1536, 512], replicated, may hold values from -0.15625 to 0.15625
Outputs:
- grad_conv_first: float32 [10, 512], replicated
- grad_norm: float32 [2, 512], replicated
- grad_conv_second: float32 [1536, 512], P('dy')
Inputs may be any that keep to these rules, and one draw needn't show every extreme that they name: In each group along dy the counts sum to 64, and some device of each group holds exactly 8 live crops.
All inputs are finite; a program needn't handle non-finite values.
Results may differ from a plain program's by a relative error of at most 0.0051.
Values may be sent and summed in bfloat16 or wider, within the bound.
A program may use at most 128 MiB of HBM per device.

v0:
```python
import math
import jax
import jax.numpy as jnp
from jax import lax
from jax.sharding import PartitionSpec as P


def gelu_cdf(value):
    return 0.5 * (1.0 + lax.erf(value * 0.7071067811865476))


def gelu_slope(value):
    return gelu_cdf(value) + value * jnp.exp(-0.5 * value * value) * 0.3989422804014327


def forward_backward(
    crop_waves, cot_rows, conv_first, norm_gain, norm_bias, conv_second, loss_scale
):
    batch_size = crop_waves.shape[0]
    frames = cot_rows.shape[1]
    first_len = 2 * frames + 1
    channels = conv_second.shape[1]
    early_taps = crop_waves[:, : 5 * first_len].reshape(batch_size, first_len, 5)
    late_taps = crop_waves[:, 5 : 5 * first_len + 5].reshape(batch_size, first_len, 5)
    patches = jnp.concatenate([early_taps, late_taps], axis=2).reshape(batch_size * first_len, 10)
    pre_norm = jnp.dot(patches, conv_first, preferred_element_type=jnp.float32).reshape(
        batch_size, first_len, channels
    )
    centre = pre_norm - jnp.mean(pre_norm, axis=1, keepdims=True)
    inv_std = lax.rsqrt(jnp.mean(centre * centre, axis=1, keepdims=True) + 1e-05)
    normed = centre * inv_std
    shifted = normed * norm_gain + norm_bias
    hidden = (shifted * gelu_cdf(shifted)).astype(jnp.bfloat16)
    two_taps = hidden[:, : 2 * frames].reshape(batch_size, frames, 2 * channels)
    third_tap = hidden[:, 2::2]
    second_rows = jnp.concatenate([two_taps, third_tap], axis=2).reshape(
        batch_size * frames, 3 * channels
    )
    pre_act = jnp.dot(second_rows, conv_second, preferred_element_type=jnp.float32)
    grad_rows = (
        loss_scale
        * cot_rows.reshape(batch_size * frames, channels).astype(jnp.float32)
        * gelu_slope(pre_act)
    ).astype(jnp.bfloat16)
    grad_cols = jnp.dot(grad_rows, conv_second.T, preferred_element_type=jnp.float32).reshape(
        batch_size, frames, 3 * channels
    )
    first_taps = grad_cols[:, :, : 2 * channels].reshape(batch_size, 2 * frames, channels)
    late_tap = jnp.stack(
        [grad_cols[:, :, 2 * channels :], jnp.zeros((batch_size, frames, channels), jnp.float32)],
        axis=2,
    ).reshape(batch_size, 2 * frames, channels)
    grad_hidden = jnp.concatenate(
        [first_taps, jnp.zeros((batch_size, 1, channels), jnp.float32)], axis=1
    )
    grad_hidden = grad_hidden + jnp.concatenate(
        [jnp.zeros((batch_size, 2, channels), jnp.float32), late_tap[:, : 2 * frames - 1]], axis=1
    )
    grad_shift = grad_hidden * gelu_slope(shifted)
    gain_grad = jnp.sum(grad_shift * normed, axis=(0, 1))
    shift_grad = jnp.sum(grad_shift, axis=(0, 1))
    grad_scaled = grad_shift * norm_gain
    grad_pre = inv_std * (
        grad_scaled
        - jnp.mean(grad_scaled, axis=1, keepdims=True)
        - normed * jnp.mean(grad_scaled * normed, axis=1, keepdims=True)
    )
    grad_pre = grad_pre.astype(jnp.bfloat16).reshape(batch_size * first_len, channels)
    grad_first = jnp.dot(patches.T, grad_pre, preferred_element_type=jnp.float32)
    return (second_rows, grad_rows, grad_first, jnp.stack([gain_grad, shift_grad]))


def on_device(audio, counts, cotangent, conv_first, norm_gain, norm_bias, conv_second):
    groups = lax.axis_size("dx")
    position = lax.axis_index("dx")
    slot_count = audio.shape[1]
    receive = cotangent.shape[1]
    frames = cotangent.shape[2]
    all_counts = lax.all_gather(counts, "dx", axis=1, tiled=True)[0]
    starts = jnp.cumsum(all_counts, dtype=jnp.int32) - all_counts
    everything = lax.all_gather(audio, "dx", axis=1, tiled=True)[0]
    wanted = jnp.arange(receive, dtype=jnp.int32) * groups + position
    holder = (
        jnp.sum((starts[None, :] <= wanted[:, None]).astype(jnp.int32), axis=1, dtype=jnp.int32) - 1
    )
    offset = wanted - starts[holder]
    crop_waves = jnp.take(everything, holder * slot_count + offset, axis=0)
    loss_scale = 1.0 / math.sqrt(groups * lax.axis_size("dy") * receive * frames)
    second_rows, grad_rows, grad_first, grad_gains = forward_backward(
        crop_waves, cotangent[0], conv_first, norm_gain, norm_bias, conv_second, loss_scale
    )
    row_share = conv_second.shape[0] // lax.axis_size("dy")
    grad_second = jnp.dot(second_rows.T, grad_rows, preferred_element_type=jnp.float32)
    summed_first, summed_gains, whole_second = lax.psum(
        (grad_first, grad_gains, grad_second), ("dx", "dy")
    )
    summed_second = lax.dynamic_slice_in_dim(
        whole_second, lax.axis_index("dy") * row_share, row_share, 0
    )
    return (summed_first, summed_gains, summed_second)


def solution(mesh):
    in_specs = (P("dy", "dx", None), P("dy", "dx"), P("dy", "dx", None, None), P(), P(), P(), P())
    out_specs = (P(), P(), P("dy", None))
    return jax.shard_map(
        on_device, mesh=mesh, in_specs=in_specs, out_specs=out_specs, check_vma=False
    )
```

profile of v0, /device:TPU:2, one launch (start us, length us, event | category | flops | bytes accessed | tf_op | source)
XLA Modules:
  0.0 583.2 jit_solution(14442549444901075429)
XLA Ops:
  8.0 1.3 dynamic-slice
  9.3 0.7 bitcast_dynamic-update-slice_fusion
  9.9 15.7 %all-reduce.3 = s32[16]{0:T(128)S(1)} all-reduce(s32[16]{0:T(128)S(1)} %bitcast_dynamic-update-slice_fusion), channel_id=1, replica_groups=mesh['dx'=16,'dy'=32] {'dx'}, use_global_device_ids=true, to_apply=%add.3 | all-reduce | flops 16 | bytes 128 | tf_op jit(solution)/shard_map/squeeze | solution.py:79
  26.1 0.6 gather_fusion
  26.8 24.8 %all_gather.7 = bf16[1,128,2570]{2,1,0:T(8,128)(2,1)S(1)} all-gather(bf16[1,8,2570]{2,1,0:T(8,128)(2,1)} %param.7), channel_id=1, replica_groups=mesh['dx'=16,'dy'=32] {'dx'}, dimensions={1}, use_global_device_ids=true | all-gather | bytes 699040 | tf_op jit(solution)/shard_map/all_gather | solution.py:81
  51.5 0.6 gather_fusion.1
  52.3 0.4 reshape.141
  52.7 0.3 copy.15
  53.0 0.4 reshape.142
  53.4 0.3 copy.16
  53.7 1.5 fusion.27
  55.2 0.6 multiply_reduce_fusion.2
  55.8 1.3 copy-done.1
  57.2 2.4 multiply_convert_fusion.1
  59.6 11.7 %slice.24 = bf16[4,256,512]{2,1,0:T(8,128)(2,1)} slice(bf16[4,513,512]{2,1,0:T(8,128)(2,1)} %multiply_convert_fusion.1), slice={[0:4:1], [2:513:2], [0:512:1]} | slice | bytes 2097152 | tf_op jit(solution)/shard_map/slice | solution.py:35
  71.2 3.1 slice.34
  74.3 1.6 convert_multiply_fusion
  75.9 4.1 concatenate.20
  80.0 5.1 fusion.11
  85.1 3.6 fusion.12
  88.7 1.8 fusion.28
  90.5 1.5 slice.36
  92.0 2.4 slice.35
  94.4 4.9 reshape.144
  99.3 3.0 stack.15
  102.4 3.4 stack.16
  105.7 6.1 %reshape.145 = f32[4,512,512]{2,1,0:T(8,128)} reshape(f32[4,256,2,512]{3,2,1,0:T(2,128)} %stack.16) | data formatting | bytes 8388608 | tf_op jit(solution)/shard_map/reshape | solution.py:52
  111.8 7.3 %multiply_reduce_fusion = (f32[512]{0:T(512)S(1)}, f32[4,512]{1,0:T(4,128)S(1)}, f32[4,512]{1,0:T(4,128)S(1)}, f32[512]{0:T(512)S(1)}, f32[4,513,512]{2,1,0:T(8,128)S(1)}) fusion(f32[4,512]{1,0:T(4,128)S(1)} %add_rsqrt_fusion, f32[4,513,512]{2,1,0:T(8,128)} %copy-done.1, f32[4,512]{1,0:T(4,128)S(1)} %broadcast_multiply_fusion.2, f32[512]{0:T(512)S(1)} %copy-done.5, ...), kind=kLoop, calls=%fused_computation.8 | loop fusion | flops 22057984 | bytes 16826368 | tf_op jit(solution)/shard_map/reduce_sum | solution.py:60
  119.2 1.4 fusion.14
  120.6 105.0 %all-reduce.4 = (f32[10,512]{1,0:T(8,128)}, f32[2,512]{1,0:T(2,128)}) all-reduce(f32[10,512]{1,0:T(8,128)S(1)} %fusion.14, f32[2,512]{1,0:T(2,128)S(1)} %pad_maximum_fusion.8), channel_id=1, replica_groups=mesh['dx'=16,'dy'=32] {'dx','dy'}, use_global_device_ids=true, to_apply=%region_6.7 | all-reduce | flops 6144 | bytes 49152 | tf_op jit(solution)/shard_map/psum | solution.py:94
  225.6 349.2 %all-reduce.7.cloned.1.call-done = f32[1536,512]{1,0:T(8,128)} async-done(((f32[1536,512]{1,0:T(8,128)}), f32[1536,512]{1,0:T(8,128)}) %all-reduce.7.cloned.1.call-update) | async-done | bytes 3145744 | tf_op jit(solution)/shard_map/psum | solution.py:94
  574.9 1.5 constant_dynamic-slice_fusion
  (39 shorter events, 0.8 us)
Async XLA Ops:
  7.2 72.8 %copy-start = (bf16[1536,512]{1,0:T(8,128)(2,1)S(1)}, bf16[1536,512]{1,0:T(8,128)(2,1)}, u32[]{:S(2)}) copy-start(bf16[1536,512]{1,0:T(8,128)(2,1)} %param.13) | copy-start | bytes 4718596
  7.2 567.7 %all-reduce.7.cloned.1.call-start = ((), (), s32[]{:S(2)}) async-start(), calls=%async_computation | async-start | bytes 6291456 | tf_op jit(solution)/shard_map/psum | solution.py:94
  53.7 3.5 copy-start.5
  53.7 3.5 copy-start.6
  55.2 2.0 copy-start.1
  59.6 14.7 %copy-start.3 = (bf16[1,4,256,512]{3,2,1,0:T(8,128)(2,1)S(1)}, bf16[1,4,256,512]{3,2,1,0:T(8,128)(2,1)}, u32[]{:S(2)}) copy-start(bf16[1,4,256,512]{3,2,1,0:T(8,128)(2,1)} %param.9) | copy-start | bytes 3145732
  80.0 5.1 copy-start.2
  80.0 5.1 copy-start.4
  105.7 13.5 %slice-start = ((s8[4259840]{0:T(1024)(128)(4,1)}), s8[65536]{0:T(1024)(128)(4,1)S(1)}, s32[]{:S(2)}) async-start(s8[4259840]{0:T(1024)(128)(4,1)} %bitcast.48), calls=%async_computation.1 | async-start | bytes 131072
  111.8 7.4 %slice-start.1 = ((s8[4259840]{0:T(1024)(128)(4,1)}), s8[4194304]{0:T(1024)(128)(4,1)S(1)}, s32[]{:S(2)}) async-start(s8[4259840]{0:T(1024)(128)(4,1)} %bitcast.48), calls=%async_computation.2 | async-start | bytes 8388608
Sparse Core Ops, SparseCore 0:
  88.8 486.0 all-reduce.6
where the time goes:
time: 584 us; the launch traced here: 583 us
  waiting for transfers between devices  349 us (60%)
  blocking collectives  145 us (25%)
  local copies, waits for them, and re-layouts  47.7 us (8%)
  between operations  15 us (3%)
  matrix products  13.3 us (2%)
  other arithmetic  12.4 us (2%)
    psum x1, waiting for transfers between devices, on_device(): lax.psum((grad_first, grad_gains, grad_second), ('dx', 'dy'))  349 us
    psum x1, blocking collectives, on_device(): lax.psum((grad_first, grad_gains, grad_second), ('dx', 'dy'))  105 us
    all_gather x1, blocking collectives, on_device(): everything = lax.all_gather(audio, 'dx', axis=1, tiled=True)[0]  24.8 us
    squeeze x1, blocking collectives, on_device(): all_counts = lax.all_gather(counts, 'dx', axis=1, tiled=True)[0]  15.7 us
  transfers between devices with their start and end apart: 1, of which 1 were waited for; matrix products, arithmetic and copies ran while one was open for 5% of the time, Pallas kernels for 0%

commit v1 on v0

--- a/solution.py
+++ b/solution.py
@@ -78,7 +78,9 @@
     frames = cotangent.shape[2]
     all_counts = lax.all_gather(counts, "dx", axis=1, tiled=True)[0]
     starts = jnp.cumsum(all_counts, dtype=jnp.int32) - all_counts
-    everything = lax.all_gather(audio, "dx", axis=1, tiled=True)[0]
+    everything = jnp.concatenate(
+        lax.all_to_all(jnp.stack([audio] * lax.axis_size("dx")), "dx", 0, 0), axis=1
+    )[0]
     wanted = jnp.arange(receive, dtype=jnp.int32) * groups + position
     holder = (
         jnp.sum((starts[None, :] <= wanted[:, None]).astype(jnp.int32), axis=1, dtype=jnp.int32) - 1

time: 584 us -> 581 us (level)
  blocking collectives: 145 us -> 126 us
  starting transfers between devices: 0.04 us -> 9.33 us
    all_gather x1 -> x0, blocking collectives: 24.8 us -> none  [on_device(): everything = lax.all_gather(audio, 'dx', axis=1, tiled=True)[0]]
    all_to_all x0 -> x1, starting transfers between devices: none -> 9.29 us  [on_device(): lax.all_to_all(jnp.stack([audio] * lax.axis_size('dx')), 'dx', 0, 0)]
  transfers between devices with their start and end apart: 1 -> 2, of which waited for: 1 -> 1; matrix products, arithmetic and copies ran while one was open for 5% -> 5% of each run, Pallas kernels for 0% -> 0%
where the time goes in v1:
time: 581 us; the launch traced here: 580 us
  waiting for transfers between devices  354 us (61%)
  blocking collectives  126 us (22%)
  local copies, waits for them, and re-layouts  48.9 us (8%)
  between operations  15 us (3%)
  other arithmetic  13.7 us (2%)
  matrix products  13.4 us (2%)
  starting transfers between devices  9.33 us (2%)
    psum x1, waiting for transfers between devices, on_device(): lax.psum((grad_first, grad_gains, grad_second), ('dx', 'dy'))  354 us
    psum x1, blocking collectives, on_device(): lax.psum((grad_first, grad_gains, grad_second), ('dx', 'dy'))  108 us
    squeeze x1, blocking collectives, on_device(): all_counts = lax.all_gather(counts, 'dx', axis=1, tiled=True)[0]  17.9 us
  transfers between devices with their start and end apart: 2, of which 1 were waited for; matrix products, arithmetic and copies ran while one was open for 5% of the time, Pallas kernels for 0%

profile of v1, /device:TPU:2, one launch (start us, length us, event | category | flops | bytes accessed | tf_op | source)
XLA Modules:
  0.0 579.5 jit_solution(9260861824900212104)
XLA Ops:
  8.0 1.3 dynamic-slice
  9.2 0.7 bitcast_dynamic-update-slice_fusion
  9.9 1.7 stack.12
  11.6 9.3 %all-to-all-start = ((bf16[16,1,8,2570]{3,2,1,0:T(8,128)(2,1)}), bf16[16,1,8,2570]{3,2,1,0:T(8,128)(2,1)S(1)}, u32[]{:S(2)}, u32[]{:S(2)}) async-start(bf16[16,1,8,2570]{3,2,1,0:T(8,128)(2,1)} %stack.12), calls=%async_computation | async-start | bytes 1376256 | tf_op jit(solution)/shard_map/all_to_all | solution.py:82
  20.9 17.9 %all-reduce.3 = s32[16]{0:T(128)S(1)} all-reduce(s32[16]{0:T(128)S(1)} %bitcast_dynamic-update-slice_fusion), channel_id=1, replica_groups=mesh['dx'=16,'dy'=32] {'dx'}, use_global_device_ids=true, to_apply=%add.3 | all-reduce | flops 16 | bytes 128 | tf_op jit(solution)/shard_map/squeeze | solution.py:79
  39.3 0.6 gather_fusion
  40.0 2.9 convert_multiply_fusion
  42.9 0.6 gather_fusion.1
  43.6 0.4 reshape.144
  44.3 0.4 reshape.145
  45.0 0.8 fusion.27
  45.8 0.6 multiply_reduce_fusion.2
  46.4 1.3 copy-done.1
  47.7 2.4 multiply_convert_fusion.1
  50.1 10.1 %slice.24 = bf16[4,256,512]{2,1,0:T(8,128)(2,1)S(1)} slice(bf16[4,513,512]{2,1,0:T(8,128)(2,1)} %multiply_convert_fusion.1), slice={[0:4:1], [2:513:2], [0:512:1]} | slice | bytes 2097152 | tf_op jit(solution)/shard_map/slice | solution.py:35
  60.3 3.1 slice.34
  63.4 4.1 concatenate.20
  67.4 4.7 fusion.11
  72.2 1.0 copy-done.6
  73.2 3.5 fusion.12
  76.7 3.0 fusion.28
  79.7 1.5 slice.36
  81.2 2.4 slice.35
  83.6 5.0 reshape.147
  88.6 3.0 stack.13
  91.6 3.4 stack.14
  95.0 6.1 %reshape.148 = f32[4,512,512]{2,1,0:T(8,128)} reshape(f32[4,256,2,512]{3,2,1,0:T(2,128)} %stack.14) | data formatting | bytes 8388608 | tf_op jit(solution)/shard_map/reshape | solution.py:52
  101.1 7.3 %multiply_reduce_fusion = (f32[512]{0:T(512)S(1)}, f32[4,512]{1,0:T(4,128)S(1)}, f32[4,512]{1,0:T(4,128)S(1)}, f32[512]{0:T(512)S(1)}, f32[4,513,512]{2,1,0:T(8,128)S(1)}) fusion(f32[4,512]{1,0:T(4,128)S(1)} %add_rsqrt_fusion, f32[4,513,512]{2,1,0:T(8,128)} %copy-done.1, f32[4,512]{1,0:T(4,128)S(1)} %broadcast_multiply_fusion.2, f32[512]{0:T(512)S(1)} %copy-done.3, ...), kind=kLoop, calls=%fused_computation.8 | loop fusion | flops 22057984 | bytes 16826368 | tf_op jit(solution)/shard_map/reduce_sum | solution.py:60
  108.5 1.4 fusion.14
  109.8 107.8 %all-reduce.4 = (f32[10,512]{1,0:T(8,128)}, f32[2,512]{1,0:T(2,128)}) all-reduce(f32[10,512]{1,0:T(8,128)S(1)} %fusion.14, f32[2,512]{1,0:T(2,128)S(1)} %pad_maximum_fusion.8), channel_id=1, replica_groups=mesh['dx'=16,'dy'=32] {'dx','dy'}, use_global_device_ids=true, to_apply=%region_6.7 | all-reduce | flops 6144 | bytes 49152 | tf_op jit(solution)/shard_map/psum | solution.py:96
  217.6 353.5 %all-reduce.7.cloned.1.call-done = f32[1536,512]{1,0:T(8,128)} async-done(((f32[1536,512]{1,0:T(8,128)}), f32[1536,512]{1,0:T(8,128)}) %all-reduce.7.cloned.1.call-update) | async-done | bytes 3145744 | tf_op jit(solution)/shard_map/psum | solution.py:96
  571.2 1.5 constant_dynamic-slice_fusion
  (41 shorter events, 1.3 us)
Async XLA Ops:
  7.2 60.3 %copy-start = (bf16[1536,512]{1,0:T(8,128)(2,1)S(1)}, bf16[1536,512]{1,0:T(8,128)(2,1)}, u32[]{:S(2)}) copy-start(bf16[1536,512]{1,0:T(8,128)(2,1)} %param.13) | copy-start | bytes 4718596
  7.2 37.8 %copy-start.4 = (bf16[10,512]{1,0:T(8,128)(2,1)S(1)}, bf16[10,512]{1,0:T(8,128)(2,1)}, u32[]{:S(2)}) copy-start(bf16[10,512]{1,0:T(8,128)(2,1)} %param.10) | copy-start | bytes 30724
  11.6 31.3 %all-to-all-start = ((bf16[16,1,8,2570]{3,2,1,0:T(8,128)(2,1)}), bf16[16,1,8,2570]{3,2,1,0:T(8,128)(2,1)S(1)}, u32[]{:S(2)}, u32[]{:S(2)}) async-start(bf16[16,1,8,2570]{3,2,1,0:T(8,128)(2,1)} %stack.12), calls=%async_computation | async-start | bytes 1376256 | tf_op jit(solution)/shard_map/all_to_all | solution.py:82
  20.9 550.3 %all-reduce.7.cloned.1.call-start = ((), (), s32[]{:S(2)}) async-start(), calls=%async_computation.1 | async-start | bytes 6291456 | tf_op jit(solution)/shard_map/psum | solution.py:96
  45.0 2.8 copy-start.3
  45.0 2.8 copy-start.5
  45.8 2.0 copy-start.1
  67.4 5.7 copy-start.2
  72.2 1.0 copy-start.6
  95.0 13.4 %slice-start = ((s8[4259840]{0:T(1024)(128)(4,1)}), s8[65536]{0:T(1024)(128)(4,1)S(1)}, s32[]{:S(2)}) async-start(s8[4259840]{0:T(1024)(128)(4,1)} %bitcast.49), calls=%async_computation.2 | async-start | bytes 131072
  101.1 7.4 %slice-start.1 = ((s8[4259840]{0:T(1024)(128)(4,1)}), s8[4194304]{0:T(1024)(128)(4,1)S(1)}, s32[]{:S(2)}) async-start(s8[4259840]{0:T(1024)(128)(4,1)} %bitcast.49), calls=%async_computation.3 | async-start | bytes 8388608
Sparse Core Ops, SparseCore 0:
  83.8 487.3 all-reduce.6

commit v2 on v0

--- a/solution.py
+++ b/solution.py
@@ -92,7 +92,7 @@
     row_share = conv_second.shape[0] // lax.axis_size("dy")
     grad_second = jnp.dot(second_rows.T, grad_rows, preferred_element_type=jnp.float32)
     summed_first, summed_gains, whole_second = lax.psum(
-        (grad_first, grad_gains, grad_second), ("dx", "dy")
+        lax.psum((grad_first, grad_gains, grad_second), "dx"), "dy"
     )
     summed_second = lax.dynamic_slice_in_dim(
         whole_second, lax.axis_index("dy") * row_share, row_share, 0

time: 584 us -> 445 us (0.76)
  the two profiles are of different devices: /device:TPU:2 before, /device:TPU:1 now
where the time goes in v2:
time: 445 us; the launch traced here: 444 us
  blocking collectives  193 us (43%)
  waiting for transfers between devices  163 us (37%)
  local copies, waits for them, and re-layouts  47.7 us (11%)
  between operations  15 us (3%)
  matrix products  13.3 us (3%)
  other arithmetic  12.4 us (3%)
    psum x1, waiting for transfers between devices, on_device(): lax.psum((grad_first, grad_gains, grad_second), 'dx')  113 us
    psum x1, blocking collectives, on_device(): lax.psum(lax.psum((grad_first, grad_gains, grad_second), 'dx'), 'dy')  103 us
    psum x1, blocking collectives, on_device(): lax.psum((grad_first, grad_gains, grad_second), 'dx')  57.9 us
    psum x1, waiting for transfers between devices, on_device(): lax.psum(lax.psum((grad_first, grad_gains, grad_second), 'dx'), 'dy')  49.9 us
    all_gather x1, blocking collectives, on_device(): everything = lax.all_gather(audio, 'dx', axis=1, tiled=True)[0]  17.5 us
    squeeze x1, blocking collectives, on_device(): all_counts = lax.all_gather(counts, 'dx', axis=1, tiled=True)[0]  13.9 us
    slice x1, local copies, waits for them, and re-layouts, forward_backward(): third_tap = hidden[:, 2::2]  11.7 us
  transfers between devices with their start and end apart: 2, of which 2 were waited for; matrix products, arithmetic and copies ran while one was open for 7% of the time, Pallas kernels for 0%

profile of v2, /device:TPU:1, one launch (start us, length us, event | category | flops | bytes accessed | tf_op | source)
XLA Modules:
  0.0 444.3 jit_solution(6062817992419718047)
XLA Ops:
  8.0 1.3 dynamic-slice
  9.3 0.7 bitcast_dynamic-update-slice_fusion
  9.9 13.9 %all-reduce.3 = s32[16]{0:T(128)S(1)} all-reduce(s32[16]{0:T(128)S(1)} %bitcast_dynamic-update-slice_fusion), channel_id=1, replica_groups=mesh['dx'=16,'dy'=32] {'dx'}, use_global_device_ids=true, to_apply=%add.3 | all-reduce | flops 16 | bytes 128 | tf_op jit(solution)/shard_map/squeeze | solution.py:79
  24.3 0.6 gather_fusion
  25.0 17.5 %all_gather.7 = bf16[1,128,2570]{2,1,0:T(8,128)(2,1)S(1)} all-gather(bf16[1,8,2570]{2,1,0:T(8,128)(2,1)} %param.7), channel_id=1, replica_groups=mesh['dx'=16,'dy'=32] {'dx'}, dimensions={1}, use_global_device_ids=true | all-gather | bytes 699040 | tf_op jit(solution)/shard_map/all_gather | solution.py:81
  42.6 0.6 gather_fusion.1
  43.3 0.4 reshape.141
  44.0 0.4 reshape.142
  44.7 1.5 fusion.27
  46.2 0.6 multiply_reduce_fusion.2
  46.8 1.3 copy-done.1
  48.2 2.4 multiply_convert_fusion.1
  50.6 11.7 %slice.24 = bf16[4,256,512]{2,1,0:T(8,128)(2,1)} slice(bf16[4,513,512]{2,1,0:T(8,128)(2,1)} %multiply_convert_fusion.1), slice={[0:4:1], [2:513:2], [0:512:1]} | slice | bytes 2097152 | tf_op jit(solution)/shard_map/slice | solution.py:35
  62.2 3.1 slice.34
  65.3 1.6 convert_multiply_fusion
  66.9 4.1 concatenate.20
  71.0 5.1 %fusion.11 = bf16[1024,512]{1,0:T(8,128)(2,1)S(1)} fusion(f32[1,4,256,512]{3,2,1,0:T(8,128)} %convert_multiply_fusion, bf16[1536,512]{1,0:T(8,128)(2,1)S(1)} %copy-done, bf16[1024,512]{1,0:T(8,128)(2,1)} %bitcast.54, bf16[1024,1024]{1,0:T(8,128)(2,1)} %concatenate.20), kind=kOutput, calls=%fused_computation.25 | convolution fusion | flops 1622147072 | bytes 7864320 | tf_op jit(solution)/shard_map/dot_general | solution.py:39
  76.1 3.6 fusion.12
  79.9 1.8 fusion.28
  81.7 1.5 slice.36
  83.2 2.4 slice.35
  85.6 4.9 %reshape.144 = f32[4,512,512]{2,1,0:T(8,128)} reshape(f32[4,256,1024]{2,1,0:T(8,128)} %slice.35) | data formatting | bytes 8388608 | tf_op jit(solution)/shard_map/reshape | solution.py:48
  90.6 3.0 stack.15
  93.6 3.4 stack.16
  97.0 6.0 %reshape.145 = f32[4,512,512]{2,1,0:T(8,128)} reshape(f32[4,256,2,512]{3,2,1,0:T(2,128)} %stack.16) | data formatting | bytes 8388608 | tf_op jit(solution)/shard_map/reshape | solution.py:52
  103.0 113.0 %all-reduce.9.cloned.1.call-done = f32[1536,512]{1,0:T(8,128)} async-done(((f32[1536,512]{1,0:T(8,128)}), f32[1536,512]{1,0:T(8,128)}) %all-reduce.9.cloned.1.call-update) | async-done | bytes 3145744 | tf_op jit(solution)/shard_map/psum | solution.py:95
  216.1 7.3 %multiply_reduce_fusion = (f32[512]{0:T(512)S(1)}, f32[4,512]{1,0:T(4,128)S(1)}, f32[4,512]{1,0:T(4,128)S(1)}, f32[512]{0:T(512)S(1)}, f32[4,513,512]{2,1,0:T(8,128)S(1)}) fusion(f32[4,512]{1,0:T(4,128)S(1)} %add_rsqrt_fusion, f32[4,513,512]{2,1,0:T(8,128)} %copy-done.1, f32[4,512]{1,0:T(4,128)S(1)} %broadcast_multiply_fusion.2, f32[512]{0:T(512)S(1)} %copy-done.5, ...), kind=kLoop, calls=%fused_computation.8 | loop fusion | flops 22057984 | bytes 16826368 | tf_op jit(solution)/shard_map/reduce_sum | solution.py:60
  223.4 1.4 fusion.14
  224.8 57.9 %all-reduce.5 = (f32[10,512]{1,0:T(8,128)S(1)}, f32[2,512]{1,0:T(2,128)S(1)}) all-reduce(f32[10,512]{1,0:T(8,128)S(1)} %fusion.14, f32[2,512]{1,0:T(2,128)S(1)} %pad_maximum_fusion.8), channel_id=1, replica_groups=mesh['dx'=16,'dy'=32] {'dx'}, use_global_device_ids=true, to_apply=%region_6.7 | all-reduce | flops 6144 | bytes 49152 | tf_op jit(solution)/shard_map/psum | solution.py:95
  282.7 103.3 %all-reduce.4 = (f32[10,512]{1,0:T(8,128)}, f32[2,512]{1,0:T(2,128)}) all-reduce(f32[10,512]{1,0:T(8,128)S(1)} %get-tuple-element.9, f32[2,512]{1,0:T(2,128)S(1)} %get-tuple-element.10), channel_id=1, replica_groups=mesh['dx'=16,'dy'=32] {'dy'}, use_global_device_ids=true, to_apply=%region_7.8 | all-reduce | flops 6144 | bytes 49152 | tf_op jit(solution)/shard_map/psum | solution.py:94
  386.0 49.9 %all-reduce.11.cloned.1.call-done = f32[1536,512]{1,0:T(8,128)} async-done(((f32[1536,512]{1,0:T(8,128)}), f32[1536,512]{1,0:T(8,128)}) %all-reduce.11.cloned.1.call-update) | async-done | bytes 3145744 | tf_op jit(solution)/shard_map/psum | solution.py:94
  435.9 1.5 constant_dynamic-slice_fusion
  (43 shorter events, 1.6 us)
Async XLA Ops:
  7.2 63.8 %copy-start = (bf16[1536,512]{1,0:T(8,128)(2,1)S(1)}, bf16[1536,512]{1,0:T(8,128)(2,1)}, u32[]{:S(2)}) copy-start(bf16[1536,512]{1,0:T(8,128)(2,1)} %param.13) | copy-start | bytes 4718596
  7.2 208.9 %all-reduce.9.cloned.1.call-start = ((), (), s32[]{:S(2)}) async-start(), calls=%async_computation | async-start | bytes 6291456 | tf_op jit(solution)/shard_map/psum | solution.py:95
  44.7 3.5 copy-start.5
  44.7 3.5 copy-start.6
  46.2 2.0 copy-start.1
  50.6 14.7 %copy-start.3 = (bf16[1,4,256,512]{3,2,1,0:T(8,128)(2,1)S(1)}, bf16[1,4,256,512]{3,2,1,0:T(8,128)(2,1)}, u32[]{:S(2)}) copy-start(bf16[1,4,256,512]{3,2,1,0:T(8,128)(2,1)} %param.9) | copy-start | bytes 3145732
  71.0 5.1 %copy-start.2 = (bf16[1024,1024]{1,0:T(8,128)(2,1)S(1)}, bf16[1024,1024]{1,0:T(8,128)(2,1)}, u32[]{:S(2)}) copy-start(bf16[1024,1024]{1,0:T(8,128)(2,1)} %concatenate.20) | copy-start | bytes 6291460
  71.0 5.1 %copy-start.4 = (bf16[4,256,512]{2,1,0:T(8,128)(2,1)S(1)}, bf16[4,256,512]{2,1,0:T(8,128)(2,1)}, u32[]{:S(2)}) copy-start(bf16[4,256,512]{2,1,0:T(8,128)(2,1)} %slice.24) | copy-start | bytes 3145732
  79.7 356.2 %all-reduce.11.cloned.1.call-start = ((), (), s32[]{:S(2)}) async-start(), calls=%async_computation.1 | async-start | bytes 6291456 | tf_op jit(solution)/shard_map/psum | solution.py:94
  216.0 7.4 %slice-start = ((s8[4259840]{0:T(1024)(128)(4,1)}), s8[65536]{0:T(1024)(128)(4,1)S(1)}, s32[]{:S(2)}) async-start(s8[4259840]{0:T(1024)(128)(4,1)} %bitcast.48), calls=%async_computation.2 | async-start | bytes 131072
  216.1 7.3 %slice-start.1 = ((s8[4259840]{0:T(1024)(128)(4,1)}), s8[4194304]{0:T(1024)(128)(4,1)S(1)}, s32[]{:S(2)}) async-start(s8[4259840]{0:T(1024)(128)(4,1)} %bitcast.48), calls=%async_computation.3 | async-start | bytes 8388608
Sparse Core Ops, SparseCore 0:
  79.8 136.1 all-reduce.8
  218.4 217.4 all-reduce.10
